TPU v7x, 32 devices: a whole 2x2x4 slice. The times are simulated.
32 devices in a mesh: prow: 8 (over y, x, core), pcol: 4 (over z).
Axes of the slice: x: 2, y: 2, z: 4, core: 2. Of those that a mesh axis runs over, the one named last changes fastest.
Arguments:
- packed: bfloat16 [6144, 6144], P('prow', 'pcol'), may hold values from -32 to 32, as said below
- tile_scales: float32 [24, 24], P('prow', 'pcol'), may hold values from 0.5 to 2
Outputs:
- factored: bfloat16 [6144, 6144], P('prow', 'pcol')
Inputs may be any that keep to these rules, and one draw needn't show every extreme that they name: `packed`: stored tile entries lie in the range below.
All inputs are finite; a program needn't handle non-finite values.
Results may differ from a plain program's by a relative error of at most 0.0065.
Values may be sent and summed in bfloat16 or wider, within the bound.
No kernel may reach another device: no remote copies, remote signals or barrier semaphores. Data moves between devices by JAX's collectives and lax.ppermute only.
A program may use at most 64 MiB of HBM per device.

v0:
```python
import functools

import jax
import jax.numpy as jnp
import numpy as np
from jax import lax
from jax.experimental import pallas as pl
from jax.experimental.pallas import tpu as pltpu
from jax.sharding import PartitionSpec as P

F32 = jnp.float32
BF16 = jnp.bfloat16
HALF = 128
EXTRA = 16


def dot_nt(a, b, precision=None):
    dims = (((1,), (1,)), ((), ()))
    return lax.dot_general(a, b, dims, precision=precision, preferred_element_type=F32)


def dot_nn(a, b, precision=None):
    dims = (((1,), (0,)), ((), ()))
    return lax.dot_general(a, b, dims, precision=precision, preferred_element_type=F32)


HIGHEST = lax.Precision.HIGHEST


def inverse_factor(a):
    n = a.shape[0]
    blocks = n // 8
    full = (8, n)
    rows = [a[8 * i : 8 * i + 8, :] for i in range(blocks)]
    lane = lax.broadcasted_iota(jnp.int32, full, 1)
    sub = lax.broadcasted_iota(jnp.int32, full, 0)

    def column(x, k):
        return jnp.broadcast_to(x[:, k : k + 1], full)

    def row(x, k):
        return jnp.broadcast_to(x[k : k + 1, :], full)

    out = []
    own = [column(rows[0], k) for k in range(8)]
    for t in range(blocks):
        base = 8 * t
        here = jnp.logical_and(lane >= base, lane < base + 8)
        s = {(j, k): row(own[k], j) for j in range(8) for k in range(j, 8)}
        c = {}
        for i in range(t + 1, blocks):
            for j in range(8):
                c[i, j] = column(rows[i], base + j)
        last = t + 1 == blocks
        if not last:
            own = [column(rows[t + 1], base + 8 + k) for k in range(8)]
        for i in range(t + 1, blocks):
            rows[i] = jnp.where(here, 0.0, rows[i])
        b = [jnp.where(here, jnp.where(lane == base + j, 1.0, 0.0), row(rows[t], j)) for j in range(8)]
        d = [] if last else [c[t + 1, j] for j in range(8)]
        m = {}
        z = []
        x = jnp.zeros(full, F32)
        for j in range(8):
            r0 = pl.reciprocal(s[j, j], approx=True)
            e = 2.0 - s[j, j] * r0
            r = r0 * e
            for k in range(j + 1, 8):
                m[j, k] = s[j, k] * r
            for k in range(j + 1, 8):
                for l in range(k, 8):
                    if k == j + 1 and l == k:
                        s[k, l] = s[k, l] - ((s[j, k] * s[j, k]) * r0) * e
                    else:
                        s[k, l] = s[k, l] - m[j, k] * s[j, l]
                b[k] = b[k] - m[j, k] * b[j]
            z.append(r * b[j])
            if not last:
                for k in range(j + 1, 8):
                    d[k] = d[k] - m[j, k] * d[j]
                w = d[j] * r
                own = [own[k] - w * row(d[j], k) for k in range(8)]
                rows[t + 1] = rows[t + 1] - d[j] * z[j]
            x = jnp.where(sub == j, lax.rsqrt(s[j, j]) * b[j], x)
        out.append(jnp.where(lane < base + 8, x, 0.0))
        if t + 2 < blocks:
            y = list(z)
            for k in range(7, 0, -1):
                for j in range(k):
                    y[j] = y[j] - m[j, k] * y[k]
            for i in range(t + 2, blocks):
                for j in range(8):
                    rows[i] = rows[i] - c[i, j] * y[j]
    return jnp.concatenate(out, axis=0)


def split(x):
    high = x.astype(BF16)
    return high, (x - high.astype(F32)).astype(BF16)


def scale_row(ref, tile, n):
    tail = ref[n:, :].astype(F32)
    return tail[3 * tile : 3 * tile + 1] + tail[3 * tile + 1 : 3 * tile + 2] + tail[3 * tile + 2 : 3 * tile + 3]


def first_half(tile, inv_ref, low_ref, rest_ref):
    x = inverse_factor(tile[:HALF, :HALF])
    factor = dot_nt(tile[HALF:, :HALF], x, HIGHEST)
    inv_ref[...] = x
    low_ref[...] = factor
    rest_ref[...] = tile[HALF:, HALF:] - dot_nt(factor, factor, HIGHEST)


def second_half(inv_ref, low_ref, rest_ref, out_ref):
    x22 = inverse_factor(rest_ref[...])
    x11 = inv_ref[...]
    x21 = -dot_nn(x22, dot_nn(low_ref[...], x11, HIGHEST), HIGHEST)
    for k, x in enumerate((x11, x21, x22)):
        out_ref[k], out_ref[k + 3] = split(x)


def scale_tail(scales, n):
    row = lax.broadcasted_iota(jnp.int32, (EXTRA, n), 0)
    total = jnp.zeros((EXTRA, n), F32)
    for t in range(scales.shape[0]):
        rest = jnp.full((EXTRA, n), scales[t, 0], F32)
        for k in range(3):
            part = rest.astype(BF16).astype(F32)
            total = jnp.where(row == 3 * t + k, part, total)
            rest = rest - part
    return total.astype(BF16)


def pack_kernel(scales, packed, message, pivot, sem):
    n = pivot.shape[1]
    tall = message.shape[0] - EXTRA
    tile_copy = pltpu.make_async_copy(packed.at[0:n, 0:n], pivot.at[0:n], sem.at[0])
    block_copy = pltpu.make_async_copy(packed.at[:, 0:n], message.at[0:tall], sem.at[1])
    tile_copy.start()
    block_copy.start()
    tail = scale_tail(scales, n)
    pivot[n:, :] = tail
    message[tall:, :] = tail
    tile_copy.wait()
    block_copy.wait()


def take(tiles, mask, target):
    for k, tile in enumerate(tiles):

        @pl.when(mask == 2 * k)
        def _(tile=tile):
            n = target.shape[0]
            target[...] = tile[:n, :].astype(F32) * scale_row(tile, 0, n)


def factor_kernel(*refs):
    tiles, out_ref, left, tile, inv, low, rest = refs[:-6], *refs[-6:]
    n = 2 * HALF
    r = lax.axis_index("prow")

    @pl.when(r % 2 == 0)
    def _():
        take(tiles, r, tile)
        take(tiles, r ^ 2, left)
        first_half(tile, inv, low, rest)
        second_half(inv, low, rest, out_ref.at[0:6])
        take(tiles, r ^ 4, tile)
        high, part = split(left[...])
        cat = join(out_ref, 0)
        both = jnp.concatenate([cat[:, :n], cat[:, :n], cat[:, n:]], axis=1)
        panel = dot_nt(jnp.concatenate([high, part, high], axis=1), both).astype(BF16)
        for k in range(4):
            i, j = divmod(k, 2)
            out_ref[12 + k] = panel[i * HALF : (i + 1) * HALF, j * HALF : (j + 1) * HALF]
        tile[...] = tile[...] - dot_nt(panel, panel)
        first_half(tile, inv, low, rest)
        second_half(inv, low, rest, out_ref.at[6:12])


def join(x, base):
    zero = jnp.zeros((HALF, HALF), BF16)
    upper = jnp.concatenate([x[base], zero, x[base + 3], zero], axis=1)
    lower = jnp.concatenate([x[base + 1], x[base + 2], x[base + 4], x[base + 5]], axis=1)
    return jnp.concatenate([upper, lower], axis=0)


VMEM = pl.BlockSpec(memory_space=pltpu.VMEM)
SMEM = pl.BlockSpec(memory_space=pltpu.SMEM)
HBM = pl.BlockSpec(memory_space=pltpu.HBM)
BLOCK = jax.ShapeDtypeStruct((HALF, HALF), F32)
PARTS = jax.ShapeDtypeStruct((6, HALF, HALF), BF16)
FACTORS = jax.ShapeDtypeStruct((16, HALF, HALF), BF16)


def factor_call(kernel, name, outs, args, specs=None, scratch=(), work=1):
    return pl.pallas_call(
        kernel,
        out_shape=outs,
        in_specs=specs or [VMEM] * len(args),
        out_specs=(VMEM,) * len(outs),
        scratch_shapes=scratch,
        compiler_params=pltpu.CompilerParams(vmem_limit_bytes=24 << 20),
        cost_estimate=pl.CostEstimate(flops=work * 5_000_000_000, bytes_accessed=1 << 20, transcendentals=0),
        name=name,
    )(*args)


def update_kernel(geometry, scales, packed, factors, factors_other, *rest):
    ratio, nr, nc, tpr, tpc, n = geometry
    here, there, mine, relayed = rest[0:2], rest[2:4], rest[4], rest[5]
    out, stored, result, block, rowp, colp, rowl, xs, sem = rest[6:]
    r = lax.axis_index("prow")
    c = lax.axis_index("pcol")
    tall = tpr * n

    reads = [pltpu.make_async_copy(packed.at[t * n : (t + 1) * n], stored.at[t], sem.at[0, t]) for t in range(tpr)]
    writes = [pltpu.make_async_copy(result.at[t], out.at[t * n : (t + 1) * n], sem.at[1, t]) for t in range(tpr)]
    for copy in reads:
        copy.start()

    def when(condition, target, value):
        @pl.when(condition)
        def _():
            target[...] = value[...]

    when(r % 2 == 0, xs, factors)
    when(r % 2 == 1, xs, factors_other)
    cat0 = join(xs, 0).T
    cat1 = join(xs, 6).T
    cat1 = jnp.concatenate([cat1[:n], cat1[:n], cat1[n:]], axis=0)
    panel = jnp.concatenate(
        [jnp.concatenate([xs[12], xs[13]], axis=1), jnp.concatenate([xs[14], xs[15]], axis=1)], axis=0
    ).T

    def solve(each):
        for t in range(tpr):
            rows = slice(t * n, (t + 1) * n)
            a0 = block[0, rows, :]
            raw0 = dot_nn(jnp.concatenate([a0, a0], axis=1), cat0)
            p0 = (raw0 * scale_row(block[0], t, tall)).astype(BF16)
            s1 = scale_row(block[1], t, tall)
            left = block[1, rows, :].astype(F32) * s1 - dot_nn(p0, panel)
            high, low = split(left)
            f1 = dot_nn(jnp.concatenate([high, low, high], axis=1), cat1)
            each(t, raw0, f1, s1, p0, f1.astype(BF16))

    same = (r % 2) == (c % 2)
    for g in range(ratio):
        when(same, block, here[g])
        when(jnp.logical_not(same), block, there[g])

        def keep_column(t, raw0, f1, s1, p0, p1, g=g):
            colp[t * ratio + g, :n, :] = p0.T
            colp[t * ratio + g, n:, :] = p1.T

        solve(keep_column)

    late = jnp.logical_and(nc == 4, jnp.where(r % 4 == 3, c == 2, c == 3))
    when(late, block, relayed)
    when(jnp.logical_not(late), block, mine)

    def keep_row(t, raw0, f1, s1, p0, p1):
        rowp[t, :, :n] = p0
        rowp[t, :, n:] = p1

        @pl.when(c == 0)
        def _():
            rowl[t] = raw0

        @pl.when(c == 1)
        def _():
            rowl[t] = f1 / s1

    solve(keep_row)

    for t in range(tpr):
        reads[t].wait()
        true_row = t * nr + r
        for q in range(tpc):
            true_col = q * nc + c
            cols = slice(q * n, (q + 1) * n)

            @pl.when(true_row < true_col)
            def _():
                result[t, :, cols] = stored[t, :, cols]

            @pl.when(jnp.logical_and(true_row >= true_col, true_col >= 2))
            def _():
                change = dot_nn(rowp[t], colp[q])
                inverse = 1.0 / jnp.full((1, n), scales[t, q], F32)
                result[t, :, cols] = (stored[t, :, cols].astype(F32) - change * inverse).astype(BF16)

            if q * nc < 2:

                @pl.when(jnp.logical_and(true_row >= true_col, true_col < 2))
                def _():
                    row = lax.broadcasted_iota(jnp.int32, (n, n), 0)
                    col = lax.broadcasted_iota(jnp.int32, (n, n), 1)
                    keep = jnp.logical_or(row >= col, true_row != true_col)
                    result[t, :, cols] = jnp.where(keep, rowl[t], 0.0).astype(BF16)

        writes[t].start()
    for copy in writes:
        copy.wait()


def update(scales, packed, arrays, nr, nc, tpr, tpc, n):
    geometry = (nr // nc, nr, nc, tpr, tpc, n)
    tall = arrays[-1].shape[1]
    return pl.pallas_call(
        functools.partial(update_kernel, geometry),
        out_shape=jax.ShapeDtypeStruct(packed.shape, BF16),
        in_specs=[SMEM, HBM] + [VMEM] * len(arrays),
        out_specs=HBM,
        scratch_shapes=[
            pltpu.VMEM((tpr, n, tpc * n), BF16),
            pltpu.VMEM((tpr, n, tpc * n), BF16),
            pltpu.VMEM((2, tall, n), BF16),
            pltpu.VMEM((tpr, n, 2 * n), BF16),
            pltpu.VMEM((tpc, 2 * n, n), BF16),
            pltpu.VMEM((tpr, n, n), F32),
            pltpu.VMEM(FACTORS.shape, BF16),
            pltpu.SemaphoreType.DMA((2, tpr)),
        ],
        compiler_params=pltpu.CompilerParams(vmem_limit_bytes=40 << 20),
        cost_estimate=pl.CostEstimate(flops=4_000_000_000, bytes_accessed=8 << 20, transcendentals=0),
        name="update_tiles",
    )(scales, packed, *arrays)


def on_device(nr, nc, packed, tile_scales):
    tpr, tpc = tile_scales.shape
    n = packed.shape[0] // tpr
    r = lax.axis_index("prow")
    c = lax.axis_index("pcol")
    def send(x, pairs):
        table = [(a * nc + b, d * nc + e) for (a, b), (d, e) in pairs]
        return lax.ppermute(x, ("prow", "pcol"), table)

    message, pivot = pl.pallas_call(
        pack_kernel,
        out_shape=(jax.ShapeDtypeStruct((tpr * n + EXTRA, n), BF16), jax.ShapeDtypeStruct((n + EXTRA, n), BF16)),
        in_specs=[SMEM, HBM],
        out_specs=(VMEM,) * 2,
        scratch_shapes=[pltpu.SemaphoreType.DMA((2,))],
        compiler_params=pltpu.CompilerParams(vmem_limit_bytes=48 << 20),
        name="pack_panel",
    )(tile_scales, pltpu.with_memory_space_constraint(packed, pltpu.HBM))

    came = []
    for k in range(nc):
        pairs = [((1, 0), (2, k)), ((1, 1), (4, (k + 1) % nc))]
        came.append(send(pivot, pairs + [((0, 0), (0, k))] * (k > 0)))
    index = jnp.where(r == 4, (c + nc - 1) % nc, c)
    tile = jnp.where((r == 0) & (c == 0), pivot, came[0])
    for k in range(1, nc):
        tile = jnp.where(index == k, came[k], tile)
    tiles = [tile]
    for mask in range(2, nr, 2):
        tiles.append(send(tile, [((a, e), (a ^ mask, e)) for a in (0, 2, 4) for e in range(nc)]))
    u = r % nc
    if nc == 4:
        first = {0: [(1, 0), (0, 2)], 1: [(0, 1), (1, 2)], 2: [(1, 2), (0, 1)], 3: [(1, 3), (0, 1)]}
        second = {0: [(1, 2), (0, 1)], 1: [(0, 2), (1, 0)], 2: [(0, 2), (1, 0)], 3: [(0, 3), (1, 0)]}
        turns = [[((a, x), (a, y)) for a in range(nr) for x, y in t[a % 4]] for t in (first, second)]
        got = [send(message, turn) for turn in turns]
        *tiles, got[0], got[1] = lax.optimization_barrier((*tiles, *got))
        swap = (u == 0) == (c >= 2)
        m0 = jnp.where(c == 0, message, jnp.where(swap, got[0], got[1]))
        m0 = jnp.where(c == 1, jnp.where(u == 0, got[1], got[0]), m0)
        m1 = jnp.where(c == 1, message, jnp.where(swap, got[1], got[0]))
        m1 = jnp.where(c == 0, jnp.where(u == 0, got[0], got[1]), m1)
        mine = jnp.stack([m0, m1])
        relayed = send(mine, [((a, 3), (a, 2)) if a % 4 == 3 else ((a, 2), (a, 3)) for a in range(nr)])
    else:
        m0 = message
        m1 = jnp.where(c == 1, message, 0)
        for k in range(1, nc):
            m0 = jnp.where(c == k, send(message, [((a, 0), (a, k)) for a in range(nr)]), m0)
        for k in range(nc):
            if k != 1:
                m1 = jnp.where(c == k, send(message, [((a, 1), (a, k)) for a in range(nr)]), m1)
        mine = jnp.stack([m0, m1])
        relayed = mine

    ratio = nr // nc
    near = []
    for mask in range(2, nr, 2):
        pairs = [((e + nc * g, e), ((e + nc * g) ^ mask, e)) for e in range(nc) for g in range(ratio)]
        near.append(send(mine, pairs))
    scratch = [pltpu.VMEM((n, n), F32)] * 2 + [pltpu.VMEM((HALF, HALF), F32)] * 3
    (factors,) = factor_call(factor_kernel, "factor_pivots", (FACTORS,), tuple(tiles), None, scratch, 4)
    factors_other = send(factors, [((a, e), (a + 1, e)) for a in range(0, nr, 2) for e in range(nc)])
    *near, _ = lax.optimization_barrier((*near, factors))
    cols = [mine] * ratio
    for k, got in enumerate(near):
        cols = [jnp.where((r ^ (c + nc * g)) // 2 == k + 1, got, cols[g]) for g in range(ratio)]
    pairs = [((a, e), (a ^ 1, e)) for a in range(nr) for e in range(nc) if a % 2 == e % 2]
    cols_other = [send(x, pairs) for x in cols]
    packed = pltpu.with_memory_space_constraint(packed, pltpu.HBM)
    arrays = (factors, factors_other, *cols, *cols_other, mine, relayed)
    return update(tile_scales, packed, arrays, nr, nc, tpr, tpc, n)


def solution(mesh):
    nr = mesh.shape["prow"]
    nc = mesh.shape["pcol"]
    return jax.shard_map(
        functools.partial(on_device, nr, nc),
        mesh=mesh,
        in_specs=(P("prow", "pcol"), P("prow", "pcol")),
        out_specs=P("prow", "pcol"),
        check_vma=False,
    )
```

profile of v0, /device:TPU:21, one launch (start us, length us, event | category | flops | bytes accessed | tf_op | source)
XLA Modules:
  0.0 74.0 jit_solution(9866544331756842354)
XLA Ops:
  0.0 0.0 copy-start
  0.0 0.7 copy-done
  0.7 1.7 %pack_panel.1 = (bf16[784,256]{1,0:T(8,128)(2,1)S(1)}, bf16[272,256]{1,0:T(8,128)(2,1)S(1)}) custom-call(f32[3,6]{1,0:T(4,128)S(1)} %copy-done, bf16[768,1536]{1,0:T(8,128)(2,1)} %packed.3), custom_call_target="tpu_custom_call" | custom-call | tf_op jit(solution)/shard_map/pack_panel/pallas_call | solution.py:342
  2.4 0.7 collective-permute-start.3
  3.0 0.7 collective-permute-start.2
  3.7 0.7 collective-permute-start.1
  4.4 0.7 collective-permute-start
  5.1 1.3 %collective-permute-start.8 = (bf16[784,256]{1,0:T(8,128)(2,1)S(1)}, bf16[784,256]{1,0:T(8,128)(2,1)S(1)}, u32[]{:S(2)}, u32[]{:S(2)}) collective-permute-start(bf16[784,256]{1,0:T(8,128)(2,1)S(1)} %get-tuple-element.17), channel_id=1, source_target_pairs={{1,2},{0,1},{4,6},{5,4},{8,10},{9,8},{12,15},{13,12},{17,18},{16,1... | collective-permute-start | bytes 1204232 | tf_op jit(solution)/shard_map/ppermute | solution.py:340
  6.4 0.0 collective-permute-done.3
  6.4 1.3 %collective-permute-start.7 = (bf16[784,256]{1,0:T(8,128)(2,1)S(1)}, bf16[784,256]{1,0:T(8,128)(2,1)S(1)}, u32[]{:S(2)}, u32[]{:S(2)}) collective-permute-start(bf16[784,256]{1,0:T(8,128)(2,1)S(1)} %get-tuple-element.17), channel_id=1, source_target_pairs={{1,0},{0,2},{4,5},{5,6},{9,10},{8,9},{13,15},{12,13},{17,16},{16,1... | collective-permute-start | bytes 1204232 | tf_op jit(solution)/shard_map/ppermute | solution.py:340
  7.7 0.0 collective-permute-done.2
  7.7 0.0 collective-permute-done.1
  7.7 0.0 collective-permute-done
  7.8 0.7 collective-permute-start.6
  8.5 0.7 collective-permute-start.5
  9.1 0.7 collective-permute-start.4
  9.9 0.0 collective-permute-done.6.refs_3_
  9.9 0.0 collective-permute-done.5.refs_2_
  9.9 0.0 collective-permute-done.4.refs_1_
  9.9 8.2 %collective-permute-done.8 = bf16[784,256]{1,0:T(8,128)(2,1)S(1)} collective-permute-done((bf16[784,256]{1,0:T(8,128)(2,1)S(1)}, bf16[784,256]{1,0:T(8,128)(2,1)S(1)}, u32[]{:S(2)}, u32[]{:S(2)}) %collective-permute-start.8) | collective-permute-done | bytes 401440 | tf_op jit(solution)/shard_map/ppermute | solution.py:340
  18.2 8.7 %collective-permute-done.7 = bf16[784,256]{1,0:T(8,128)(2,1)S(1)} collective-permute-done((bf16[784,256]{1,0:T(8,128)(2,1)S(1)}, bf16[784,256]{1,0:T(8,128)(2,1)S(1)}, u32[]{:S(2)}, u32[]{:S(2)}) %collective-permute-start.7) | collective-permute-done | bytes 401440 | tf_op jit(solution)/shard_map/ppermute | solution.py:340
  26.9 0.1 select_bitcast_fusion.1
  27.0 0.1 pad_maximum_fusion.rest_4_
  27.1 1.3 %collective-permute-start.15 = (bf16[2,784,256]{2,1,0:T(8,128)(2,1)S(1)}, bf16[2,784,256]{2,1,0:T(8,128)(2,1)S(1)}, u32[]{:S(2)}, u32[]{:S(2)}) collective-permute-start(bf16[2,784,256]{2,1,0:T(8,128)(2,1)S(1)} %pad_maximum_fusion.rest_4_), channel_id=1, source_target_pairs={{2,3},{6,7},{10,11},{15,14},{18,19},{22,23},{26,27},{31,30}} | collective-permute-start | bytes 2408456 | tf_op jit(solution)/shard_map/ppermute | solution.py:340
  28.5 0.7 collective-permute-start.12
  29.2 0.7 collective-permute-start.11
  29.9 0.7 collective-permute-start.10
  30.6 0.2 factor_pivots.1.factors
  30.9 0.0 copy-start.1
  30.9 0.0 collective-permute-done.12
  30.9 0.0 collective-permute-done.11
  30.9 0.0 collective-permute-done.10
  30.9 0.2 select_select_fusion
  31.1 1.3 %collective-permute-start.14 = (bf16[2,784,256]{2,1,0:T(8,128)(2,1)S(1)}, bf16[2,784,256]{2,1,0:T(8,128)(2,1)S(1)}, u32[]{:S(2)}, u32[]{:S(2)}) collective-permute-start(bf16[2,784,256]{2,1,0:T(8,128)(2,1)S(1)} %get-tuple-element.27.rest_1_), channel_id=1, source_target_pairs={{0,4},{2,6},{5,1},{7,3},{8,12},{10,14},{13,9},{15,11},{16,20},{18,... | collective-permute-start | bytes 2408456 | tf_op jit(solution)/shard_map/ppermute | solution.py:340
  32.4 1.3 %collective-permute-start.13 = (bf16[2,784,256]{2,1,0:T(8,128)(2,1)S(1)}, bf16[2,784,256]{2,1,0:T(8,128)(2,1)S(1)}, u32[]{:S(2)}, u32[]{:S(2)}) collective-permute-start(bf16[2,784,256]{2,1,0:T(8,128)(2,1)S(1)} %get-tuple-element.28.rest_0_), channel_id=1, source_target_pairs={{0,4},{2,6},{5,1},{7,3},{8,12},{10,14},{13,9},{15,11},{16,20},{18,... | collective-permute-start | bytes 2408456 | tf_op jit(solution)/shard_map/ppermute | solution.py:340
  33.7 1.3 %collective-permute-start.9 = (bf16[16,128,128]{2,1,0:T(8,128)(2,1)S(1)}, bf16[16,128,128]{2,1,0:T(8,128)(2,1)S(1)}, u32[]{:S(2)}, u32[]{:S(2)}) collective-permute-start(bf16[16,128,128]{2,1,0:T(8,128)(2,1)S(1)} %factor_pivots.1.factors), channel_id=1, source_target_pairs={{0,4},{1,5},{2,6},{3,7},{8,12},{9,13},{10,14},{11,15},{16,20},{17,... | collective-permute-start | bytes 1572872 | tf_op jit(solution)/shard_map/ppermute | solution.py:340
  35.0 30.2 %collective-permute-done.9.factors_other = bf16[16,128,128]{2,1,0:T(8,128)(2,1)S(1)} collective-permute-done((bf16[16,128,128]{2,1,0:T(8,128)(2,1)S(1)}, bf16[16,128,128]{2,1,0:T(8,128)(2,1)S(1)}, u32[]{:S(2)}, u32[]{:S(2)}) %collective-permute-start.9) | collective-permute-done | bytes 524320 | tf_op jit(solution)/shard_map/ppermute | solution.py:340
  65.2 0.0 collective-permute-done.15.rest_5_
  65.2 0.0 collective-permute-done.14.rest_3_
  65.2 0.0 collective-permute-done.13.rest_2_
  65.2 0.0 copy-done.1
  65.2 8.6 %update_tiles.1 = bf16[768,1536]{1,0:T(8,128)(2,1)} custom-call(f32[3,6]{1,0:T(4,128)S(1)} %copy-done.1, bf16[768,1536]{1,0:T(8,128)(2,1)} %packed.3, bf16[16,128,128]{2,1,0:T(8,128)(2,1)S(1)} %factor_pivots.1.factors, bf16[16,128,128]{2,1,0:T(8,128)(2,1)S(1)} %collective-permute-done.9.factors_other, bf16[2,784,256]{2,1,0:T(8,128)(2,1)S(1)} %get-tuple-element.28.rest_0_, ...), custom_call_target="tpu_custom_call" | custom-call | flops 4000000000 | bytes 8388608 | tf_op jit(solution)/shard_map/update_tiles/pallas_call | solution.py:312
  (1 shorter events, 0.0 us)
Async XLA Ops:
  0.0 0.7 copy-start
  2.4 4.0 %collective-permute-start.3 = (bf16[272,256]{1,0:T(8,128)(2,1)S(1)}, bf16[272,256]{1,0:T(8,128)(2,1)S(1)}, u32[]{:S(2)}, u32[]{:S(2)}) collective-permute-start(bf16[272,256]{1,0:T(8,128)(2,1)S(1)} %get-tuple-element.16), channel_id=1, source_target_pairs={{4,8},{5,17}} | collective-permute-start | bytes 417800 | tf_op jit(solution)/shard_map/ppermute | solution.py:340
  3.0 4.7 %collective-permute-start.2 = (bf16[272,256]{1,0:T(8,128)(2,1)S(1)}, bf16[272,256]{1,0:T(8,128)(2,1)S(1)}, u32[]{:S(2)}, u32[]{:S(2)}) collective-permute-start(bf16[272,256]{1,0:T(8,128)(2,1)S(1)} %get-tuple-element.16), channel_id=1, source_target_pairs={{4,9},{5,18},{0,1}} | collective-permute-start | bytes 417800 | tf_op jit(solution)/shard_map/ppermute | solution.py:340
  3.7 4.0 %collective-permute-start.1 = (bf16[272,256]{1,0:T(8,128)(2,1)S(1)}, bf16[272,256]{1,0:T(8,128)(2,1)S(1)}, u32[]{:S(2)}, u32[]{:S(2)}) collective-permute-start(bf16[272,256]{1,0:T(8,128)(2,1)S(1)} %get-tuple-element.16), channel_id=1, source_target_pairs={{4,10},{5,19},{0,2}} | collective-permute-start | bytes 417800 | tf_op jit(solution)/shard_map/ppermute | solution.py:340
  4.4 3.3 %collective-permute-start = (bf16[272,256]{1,0:T(8,128)(2,1)S(1)}, bf16[272,256]{1,0:T(8,128)(2,1)S(1)}, u32[]{:S(2)}, u32[]{:S(2)}) collective-permute-start(bf16[272,256]{1,0:T(8,128)(2,1)S(1)} %get-tuple-element.16), channel_id=1, source_target_pairs={{4,11},{5,16},{0,3}} | collective-permute-start | bytes 417800 | tf_op jit(solution)/shard_map/ppermute | solution.py:340
  5.1 13.1 %collective-permute-start.8 = (bf16[784,256]{1,0:T(8,128)(2,1)S(1)}, bf16[784,256]{1,0:T(8,128)(2,1)S(1)}, u32[]{:S(2)}, u32[]{:S(2)}) collective-permute-start(bf16[784,256]{1,0:T(8,128)(2,1)S(1)} %get-tuple-element.17), channel_id=1, source_target_pairs={{1,2},{0,1},{4,6},{5,4},{8,10},{9,8},{12,15},{13,12},{17,18},{16,1... | collective-permute-start | bytes 1204232 | tf_op jit(solution)/shard_map/ppermute | solution.py:340
  6.4 20.5 %collective-permute-start.7 = (bf16[784,256]{1,0:T(8,128)(2,1)S(1)}, bf16[784,256]{1,0:T(8,128)(2,1)S(1)}, u32[]{:S(2)}, u32[]{:S(2)}) collective-permute-start(bf16[784,256]{1,0:T(8,128)(2,1)S(1)} %get-tuple-element.17), channel_id=1, source_target_pairs={{1,0},{0,2},{4,5},{5,6},{9,10},{8,9},{13,15},{12,13},{17,16},{16,1... | collective-permute-start | bytes 1204232 | tf_op jit(solution)/shard_map/ppermute | solution.py:340
  7.8 2.1 %collective-permute-start.6 = (bf16[272,256]{1,0:T(8,128)(2,1)S(1)}, bf16[272,256]{1,0:T(8,128)(2,1)S(1)}, u32[]{:S(2)}, u32[]{:S(2)}) collective-permute-start(bf16[272,256]{1,0:T(8,128)(2,1)S(1)} %select_select_fusion.2.refs_0_), channel_id=1, source_target_pairs={{0,24},{1,25},{2,26},{3,27},{8,16},{9,17},{10,18},{11,19},{16,8},{... | collective-permute-start | bytes 417800 | tf_op jit(solution)/shard_map/ppermute | solution.py:340
  8.5 1.4 %collective-permute-start.5 = (bf16[272,256]{1,0:T(8,128)(2,1)S(1)}, bf16[272,256]{1,0:T(8,128)(2,1)S(1)}, u32[]{:S(2)}, u32[]{:S(2)}) collective-permute-start(bf16[272,256]{1,0:T(8,128)(2,1)S(1)} %select_select_fusion.2.refs_0_), channel_id=1, source_target_pairs={{0,16},{1,17},{2,18},{3,19},{8,24},{9,25},{10,26},{11,27},{16,0},{... | collective-permute-start | bytes 417800 | tf_op jit(solution)/shard_map/ppermute | solution.py:340
  9.1 0.8 %collective-permute-start.4 = (bf16[272,256]{1,0:T(8,128)(2,1)S(1)}, bf16[272,256]{1,0:T(8,128)(2,1)S(1)}, u32[]{:S(2)}, u32[]{:S(2)}) collective-permute-start(bf16[272,256]{1,0:T(8,128)(2,1)S(1)} %select_select_fusion.2.refs_0_), channel_id=1, source_target_pairs={{0,8},{1,9},{2,10},{3,11},{8,0},{9,1},{10,2},{11,3},{16,24},{17,25... | collective-permute-start | bytes 417800 | tf_op jit(solution)/shard_map/ppermute | solution.py:340
  27.1 38.1 %collective-permute-start.15 = (bf16[2,784,256]{2,1,0:T(8,128)(2,1)S(1)}, bf16[2,784,256]{2,1,0:T(8,128)(2,1)S(1)}, u32[]{:S(2)}, u32[]{:S(2)}) collective-permute-start(bf16[2,784,256]{2,1,0:T(8,128)(2,1)S(1)} %pad_maximum_fusion.rest_4_), channel_id=1, source_target_pairs={{2,3},{6,7},{10,11},{15,14},{18,19},{22,23},{26,27},{31,30}} | collective-permute-start | bytes 2408456 | tf_op jit(solution)/shard_map/ppermute | solution.py:340
  28.5 2.4 %collective-permute-start.12 = (bf16[2,784,256]{2,1,0:T(8,128)(2,1)S(1)}, bf16[2,784,256]{2,1,0:T(8,128)(2,1)S(1)}, u32[]{:S(2)}, u32[]{:S(2)}) collective-permute-start(bf16[2,784,256]{2,1,0:T(8,128)(2,1)S(1)} %pad_maximum_fusion.rest_4_), channel_id=1, source_target_pairs={{0,24},{16,8},{5,29},{21,13},{10,18},{26,2},{15,23},{31,7}} | collective-permute-start | bytes 2408456 | tf_op jit(solution)/shard_map/ppermute | solution.py:340
  29.2 1.7 %collective-permute-start.11 = (bf16[2,784,256]{2,1,0:T(8,128)(2,1)S(1)}, bf16[2,784,256]{2,1,0:T(8,128)(2,1)S(1)}, u32[]{:S(2)}, u32[]{:S(2)}) collective-permute-start(bf16[2,784,256]{2,1,0:T(8,128)(2,1)S(1)} %pad_maximum_fusion.rest_4_), channel_id=1, source_target_pairs={{0,16},{16,0},{5,21},{21,5},{10,26},{26,10},{15,31},{31,15}} | collective-permute-start | bytes 2408456 | tf_op jit(solution)/shard_map/ppermute | solution.py:340
  29.9 1.0 %collective-permute-start.10 = (bf16[2,784,256]{2,1,0:T(8,128)(2,1)S(1)}, bf16[2,784,256]{2,1,0:T(8,128)(2,1)S(1)}, u32[]{:S(2)}, u32[]{:S(2)}) collective-permute-start(bf16[2,784,256]{2,1,0:T(8,128)(2,1)S(1)} %pad_maximum_fusion.rest_4_), channel_id=1, source_target_pairs={{0,8},{16,24},{5,13},{21,29},{10,2},{26,18},{15,7},{31,23}} | collective-permute-start | bytes 2408456 | tf_op jit(solution)/shard_map/ppermute | solution.py:340
  30.9 34.3 %copy-start.1 = (f32[3,6]{1,0:T(4,128)S(1)}, f32[3,6]{1,0:T(4,128)}, u32[]{:S(2)}) copy-start(f32[3,6]{1,0:T(4,128)} %scales.3) | copy-start | bytes 220
  31.1 34.1 %collective-permute-start.14 = (bf16[2,784,256]{2,1,0:T(8,128)(2,1)S(1)}, bf16[2,784,256]{2,1,0:T(8,128)(2,1)S(1)}, u32[]{:S(2)}, u32[]{:S(2)}) collective-permute-start(bf16[2,784,256]{2,1,0:T(8,128)(2,1)S(1)} %get-tuple-element.27.rest_1_), channel_id=1, source_target_pairs={{0,4},{2,6},{5,1},{7,3},{8,12},{10,14},{13,9},{15,11},{16,20},{18,... | collective-permute-start | bytes 2408456 | tf_op jit(solution)/shard_map/ppermute | solution.py:340
  32.4 32.8 %collective-permute-start.13 = (bf16[2,784,256]{2,1,0:T(8,128)(2,1)S(1)}, bf16[2,784,256]{2,1,0:T(8,128)(2,1)S(1)}, u32[]{:S(2)}, u32[]{:S(2)}) collective-permute-start(bf16[2,784,256]{2,1,0:T(8,128)(2,1)S(1)} %get-tuple-element.28.rest_0_), channel_id=1, source_target_pairs={{0,4},{2,6},{5,1},{7,3},{8,12},{10,14},{13,9},{15,11},{16,20},{18,... | collective-permute-start | bytes 2408456 | tf_op jit(solution)/shard_map/ppermute | solution.py:340
  33.7 31.5 %collective-permute-start.9 = (bf16[16,128,128]{2,1,0:T(8,128)(2,1)S(1)}, bf16[16,128,128]{2,1,0:T(8,128)(2,1)S(1)}, u32[]{:S(2)}, u32[]{:S(2)}) collective-permute-start(bf16[16,128,128]{2,1,0:T(8,128)(2,1)S(1)} %factor_pivots.1.factors), channel_id=1, source_target_pairs={{0,4},{1,5},{2,6},{3,7},{8,12},{9,13},{10,14},{11,15},{16,20},{17,... | collective-permute-start | bytes 1572872 | tf_op jit(solution)/shard_map/ppermute | solution.py:340
where the time goes:
time: 74.5 us; the launch traced here: 74 us
  waiting for transfers between devices  47.2 us (63%)
  starting transfers between devices  14.6 us (20%)
  Pallas kernels  10.5 us (14%)
    ppermute x16, waiting for transfers between devices, send(): return lax.ppermute(x, ('prow', 'pcol'), table)  47.2 us
    ppermute x16, starting transfers between devices, send(): return lax.ppermute(x, ('prow', 'pcol'), table)  14.6 us
    pallas_call x1, Pallas kernels, update(): pl.pallas_call(functools.partial(update_kernel, geometry), out_shape=jax....  8.63 us
    pallas_call x1, Pallas kernels, on_device(): pl.pallas_call(pack_kernel, out_shape=(jax.ShapeDtypeStruct((tpr * n + EX...  1.66 us
  transfers between devices with their start and end apart: 16, of which 3 were waited for; matrix products, arithmetic and copies ran while one was open for 0% of the time, Pallas kernels for 0%

commit v1 on v0

--- a/solution.py
+++ b/solution.py
@@ -112,10 +112,16 @@
     rest_ref[...] = tile[HALF:, HALF:] - dot_nt(factor, factor, HIGHEST)
 
 
+def dot_parts(a, b):
+    ah, al = split(a)
+    bh, bl = split(b)
+    return dot_nn(jnp.concatenate([ah, al, ah], axis=1), jnp.concatenate([bh, bh, bl], axis=0))
+
+
 def second_half(inv_ref, low_ref, rest_ref, out_ref):
     x22 = inverse_factor(rest_ref[...])
     x11 = inv_ref[...]
-    x21 = -dot_nn(x22, dot_nn(low_ref[...], x11, HIGHEST), HIGHEST)
+    x21 = -dot_parts(x22, dot_parts(low_ref[...], x11))
     for k, x in enumerate((x11, x21, x22)):
         out_ref[k], out_ref[k + 3] = split(x)
 
@@ -347,7 +353,7 @@
         scratch_shapes=[pltpu.SemaphoreType.DMA((2,))],
         compiler_params=pltpu.CompilerParams(vmem_limit_bytes=48 << 20),
         name="pack_panel",
-    )(tile_scales, pltpu.with_memory_space_constraint(packed, pltpu.HBM))
+    )(pltpu.with_memory_space_constraint(tile_scales, pltpu.HBM), pltpu.with_memory_space_constraint(packed, pltpu.HBM))
 
     came = []
     for k in range(nc):

time: 74.5 us -> 73.9 us (level)
  no operation moved by 1% of the time
where the time goes in v1:
time: 73.9 us; the launch traced here: 73.5 us
  waiting for transfers between devices  47.2 us (64%)
  starting transfers between devices  14.6 us (20%)
  Pallas kernels  10.7 us (14%)
    ppermute x16, waiting for transfers between devices, send(): return lax.ppermute(x, ('prow', 'pcol'), table)  47.2 us
    ppermute x16, starting transfers between devices, send(): return lax.ppermute(x, ('prow', 'pcol'), table)  14.6 us
    pallas_call x1, Pallas kernels, update(): pl.pallas_call(functools.partial(update_kernel, geometry), out_shape=jax....  8.63 us
    pallas_call x1, Pallas kernels, on_device(): pl.pallas_call(pack_kernel, out_shape=(jax.ShapeDtypeStruct((tpr * n + EX...  1.78 us
  transfers between devices with their start and end apart: 16, of which 3 were waited for; matrix products, arithmetic and copies ran while one was open for 0% of the time, Pallas kernels for 0%

profile of v1, /device:TPU:21, one launch (start us, length us, event | category | flops | bytes accessed | tf_op | source)
XLA Modules:
  0.0 73.5 jit_solution(8107015729627183599)
XLA Ops:
  0.0 1.8 %pack_panel.1 = (bf16[784,256]{1,0:T(8,128)(2,1)S(1)}, bf16[272,256]{1,0:T(8,128)(2,1)S(1)}) custom-call(f32[3,6]{1,0:T(4,128)} %scales.3, bf16[768,1536]{1,0:T(8,128)(2,1)} %packed.3), custom_call_target="tpu_custom_call" | custom-call | tf_op jit(solution)/shard_map/pack_panel/pallas_call | solution.py:348
  1.8 0.7 collective-permute-start.3
  2.5 0.7 collective-permute-start.2
  3.1 0.7 collective-permute-start.1
  3.8 0.7 collective-permute-start
  4.5 1.3 %collective-permute-start.8 = (bf16[784,256]{1,0:T(8,128)(2,1)S(1)}, bf16[784,256]{1,0:T(8,128)(2,1)S(1)}, u32[]{:S(2)}, u32[]{:S(2)}) collective-permute-start(bf16[784,256]{1,0:T(8,128)(2,1)S(1)} %get-tuple-element.17), channel_id=1, source_target_pairs={{1,2},{0,1},{4,6},{5,4},{8,10},{9,8},{12,15},{13,12},{17,18},{16,1... | collective-permute-start | bytes 1204232 | tf_op jit(solution)/shard_map/ppermute | solution.py:346
  5.8 0.0 collective-permute-done.3
  5.8 1.3 %collective-permute-start.7 = (bf16[784,256]{1,0:T(8,128)(2,1)S(1)}, bf16[784,256]{1,0:T(8,128)(2,1)S(1)}, u32[]{:S(2)}, u32[]{:S(2)}) collective-permute-start(bf16[784,256]{1,0:T(8,128)(2,1)S(1)} %get-tuple-element.17), channel_id=1, source_target_pairs={{1,0},{0,2},{4,5},{5,6},{9,10},{8,9},{13,15},{12,13},{17,16},{16,1... | collective-permute-start | bytes 1204232 | tf_op jit(solution)/shard_map/ppermute | solution.py:346
  7.1 0.0 collective-permute-done.2
  7.2 0.0 collective-permute-done.1
  7.2 0.0 collective-permute-done
  7.2 0.7 collective-permute-start.6
  7.9 0.7 collective-permute-start.5
  8.6 0.7 collective-permute-start.4
  9.3 0.0 collective-permute-done.6.refs_3_
  9.3 0.0 collective-permute-done.5.refs_2_
  9.4 0.0 collective-permute-done.4.refs_1_
  9.4 8.2 %collective-permute-done.8 = bf16[784,256]{1,0:T(8,128)(2,1)S(1)} collective-permute-done((bf16[784,256]{1,0:T(8,128)(2,1)S(1)}, bf16[784,256]{1,0:T(8,128)(2,1)S(1)}, u32[]{:S(2)}, u32[]{:S(2)}) %collective-permute-start.8) | collective-permute-done | bytes 401440 | tf_op jit(solution)/shard_map/ppermute | solution.py:346
  17.6 8.7 %collective-permute-done.7 = bf16[784,256]{1,0:T(8,128)(2,1)S(1)} collective-permute-done((bf16[784,256]{1,0:T(8,128)(2,1)S(1)}, bf16[784,256]{1,0:T(8,128)(2,1)S(1)}, u32[]{:S(2)}, u32[]{:S(2)}) %collective-permute-start.7) | collective-permute-done | bytes 401440 | tf_op jit(solution)/shard_map/ppermute | solution.py:346
  26.3 0.1 select_bitcast_fusion.1
  26.5 0.1 pad_maximum_fusion.rest_4_
  26.5 1.3 %collective-permute-start.15 = (bf16[2,784,256]{2,1,0:T(8,128)(2,1)S(1)}, bf16[2,784,256]{2,1,0:T(8,128)(2,1)S(1)}, u32[]{:S(2)}, u32[]{:S(2)}) collective-permute-start(bf16[2,784,256]{2,1,0:T(8,128)(2,1)S(1)} %pad_maximum_fusion.rest_4_), channel_id=1, source_target_pairs={{2,3},{6,7},{10,11},{15,14},{18,19},{22,23},{26,27},{31,30}} | collective-permute-start | bytes 2408456 | tf_op jit(solution)/shard_map/ppermute | solution.py:346
  27.9 0.7 collective-permute-start.12
  28.6 0.7 collective-permute-start.11
  29.3 0.7 collective-permute-start.10
  30.1 0.2 factor_pivots.1.factors
  30.3 0.0 copy-start
  30.3 0.0 collective-permute-done.12
  30.3 0.0 collective-permute-done.11
  30.3 0.0 collective-permute-done.10
  30.3 0.2 select_select_fusion
  30.6 1.3 %collective-permute-start.14 = (bf16[2,784,256]{2,1,0:T(8,128)(2,1)S(1)}, bf16[2,784,256]{2,1,0:T(8,128)(2,1)S(1)}, u32[]{:S(2)}, u32[]{:S(2)}) collective-permute-start(bf16[2,784,256]{2,1,0:T(8,128)(2,1)S(1)} %get-tuple-element.27.rest_1_), channel_id=1, source_target_pairs={{0,4},{2,6},{5,1},{7,3},{8,12},{10,14},{13,9},{15,11},{16,20},{18,... | collective-permute-start | bytes 2408456 | tf_op jit(solution)/shard_map/ppermute | solution.py:346
  31.9 1.3 %collective-permute-start.13 = (bf16[2,784,256]{2,1,0:T(8,128)(2,1)S(1)}, bf16[2,784,256]{2,1,0:T(8,128)(2,1)S(1)}, u32[]{:S(2)}, u32[]{:S(2)}) collective-permute-start(bf16[2,784,256]{2,1,0:T(8,128)(2,1)S(1)} %get-tuple-element.28.rest_0_), channel_id=1, source_target_pairs={{0,4},{2,6},{5,1},{7,3},{8,12},{10,14},{13,9},{15,11},{16,20},{18,... | collective-permute-start | bytes 2408456 | tf_op jit(solution)/shard_map/ppermute | solution.py:346
  33.2 1.3 %collective-permute-start.9 = (bf16[16,128,128]{2,1,0:T(8,128)(2,1)S(1)}, bf16[16,128,128]{2,1,0:T(8,128)(2,1)S(1)}, u32[]{:S(2)}, u32[]{:S(2)}) collective-permute-start(bf16[16,128,128]{2,1,0:T(8,128)(2,1)S(1)} %factor_pivots.1.factors), channel_id=1, source_target_pairs={{0,4},{1,5},{2,6},{3,7},{8,12},{9,13},{10,14},{11,15},{16,20},{17,... | collective-permute-start | bytes 1572872 | tf_op jit(solution)/shard_map/ppermute | solution.py:346
  34.5 30.2 %collective-permute-done.9.factors_other = bf16[16,128,128]{2,1,0:T(8,128)(2,1)S(1)} collective-permute-done((bf16[16,128,128]{2,1,0:T(8,128)(2,1)S(1)}, bf16[16,128,128]{2,1,0:T(8,128)(2,1)S(1)}, u32[]{:S(2)}, u32[]{:S(2)}) %collective-permute-start.9) | collective-permute-done | bytes 524320 | tf_op jit(solution)/shard_map/ppermute | solution.py:346
  64.6 0.0 collective-permute-done.15.rest_5_
  64.6 0.0 collective-permute-done.14.rest_3_
  64.6 0.0 collective-permute-done.13.rest_2_
  64.6 0.0 copy-done
  64.7 8.6 %update_tiles.1 = bf16[768,1536]{1,0:T(8,128)(2,1)} custom-call(f32[3,6]{1,0:T(4,128)S(1)} %copy-done, bf16[768,1536]{1,0:T(8,128)(2,1)} %packed.3, bf16[16,128,128]{2,1,0:T(8,128)(2,1)S(1)} %factor_pivots.1.factors, bf16[16,128,128]{2,1,0:T(8,128)(2,1)S(1)} %collective-permute-done.9.factors_other, bf16[2,784,256]{2,1,0:T(8,128)(2,1)S(1)} %get-tuple-element.28.rest_0_, ...), custom_call_target="tpu_custom_call" | custom-call | flops 4000000000 | bytes 8388608 | tf_op jit(solution)/shard_map/update_tiles/pallas_call | solution.py:318
  (1 shorter events, 0.0 us)
Async XLA Ops:
  1.8 4.0 %collective-permute-start.3 = (bf16[272,256]{1,0:T(8,128)(2,1)S(1)}, bf16[272,256]{1,0:T(8,128)(2,1)S(1)}, u32[]{:S(2)}, u32[]{:S(2)}) collective-permute-start(bf16[272,256]{1,0:T(8,128)(2,1)S(1)} %get-tuple-element.16), channel_id=1, source_target_pairs={{4,8},{5,17}} | collective-permute-start | bytes 417800 | tf_op jit(solution)/shard_map/ppermute | solution.py:346
  2.5 4.7 %collective-permute-start.2 = (bf16[272,256]{1,0:T(8,128)(2,1)S(1)}, bf16[272,256]{1,0:T(8,128)(2,1)S(1)}, u32[]{:S(2)}, u32[]{:S(2)}) collective-permute-start(bf16[272,256]{1,0:T(8,128)(2,1)S(1)} %get-tuple-element.16), channel_id=1, source_target_pairs={{4,9},{5,18},{0,1}} | collective-permute-start | bytes 417800 | tf_op jit(solution)/shard_map/ppermute | solution.py:346
  3.1 4.0 %collective-permute-start.1 = (bf16[272,256]{1,0:T(8,128)(2,1)S(1)}, bf16[272,256]{1,0:T(8,128)(2,1)S(1)}, u32[]{:S(2)}, u32[]{:S(2)}) collective-permute-start(bf16[272,256]{1,0:T(8,128)(2,1)S(1)} %get-tuple-element.16), channel_id=1, source_target_pairs={{4,10},{5,19},{0,2}} | collective-permute-start | bytes 417800 | tf_op jit(solution)/shard_map/ppermute | solution.py:346
  3.8 3.3 %collective-permute-start = (bf16[272,256]{1,0:T(8,128)(2,1)S(1)}, bf16[272,256]{1,0:T(8,128)(2,1)S(1)}, u32[]{:S(2)}, u32[]{:S(2)}) collective-permute-start(bf16[272,256]{1,0:T(8,128)(2,1)S(1)} %get-tuple-element.16), channel_id=1, source_target_pairs={{4,11},{5,16},{0,3}} | collective-permute-start | bytes 417800 | tf_op jit(solution)/shard_map/ppermute | solution.py:346
  4.5 13.1 %collective-permute-start.8 = (bf16[784,256]{1,0:T(8,128)(2,1)S(1)}, bf16[784,256]{1,0:T(8,128)(2,1)S(1)}, u32[]{:S(2)}, u32[]{:S(2)}) collective-permute-start(bf16[784,256]{1,0:T(8,128)(2,1)S(1)} %get-tuple-element.17), channel_id=1, source_target_pairs={{1,2},{0,1},{4,6},{5,4},{8,10},{9,8},{12,15},{13,12},{17,18},{16,1... | collective-permute-start | bytes 1204232 | tf_op jit(solution)/shard_map/ppermute | solution.py:346
  5.8 20.5 %collective-permute-start.7 = (bf16[784,256]{1,0:T(8,128)(2,1)S(1)}, bf16[784,256]{1,0:T(8,128)(2,1)S(1)}, u32[]{:S(2)}, u32[]{:S(2)}) collective-permute-start(bf16[784,256]{1,0:T(8,128)(2,1)S(1)} %get-tuple-element.17), channel_id=1, source_target_pairs={{1,0},{0,2},{4,5},{5,6},{9,10},{8,9},{13,15},{12,13},{17,16},{16,1... | collective-permute-start | bytes 1204232 | tf_op jit(solution)/shard_map/ppermute | solution.py:346
  7.2 2.1 %collective-permute-start.6 = (bf16[272,256]{1,0:T(8,128)(2,1)S(1)}, bf16[272,256]{1,0:T(8,128)(2,1)S(1)}, u32[]{:S(2)}, u32[]{:S(2)}) collective-permute-start(bf16[272,256]{1,0:T(8,128)(2,1)S(1)} %select_select_fusion.2.refs_0_), channel_id=1, source_target_pairs={{0,24},{1,25},{2,26},{3,27},{8,16},{9,17},{10,18},{11,19},{16,8},{... | collective-permute-start | bytes 417800 | tf_op jit(solution)/shard_map/ppermute | solution.py:346
  7.9 1.4 %collective-permute-start.5 = (bf16[272,256]{1,0:T(8,128)(2,1)S(1)}, bf16[272,256]{1,0:T(8,128)(2,1)S(1)}, u32[]{:S(2)}, u32[]{:S(2)}) collective-permute-start(bf16[272,256]{1,0:T(8,128)(2,1)S(1)} %select_select_fusion.2.refs_0_), channel_id=1, source_target_pairs={{0,16},{1,17},{2,18},{3,19},{8,24},{9,25},{10,26},{11,27},{16,0},{... | collective-permute-start | bytes 417800 | tf_op jit(solution)/shard_map/ppermute | solution.py:346
  8.6 0.8 %collective-permute-start.4 = (bf16[272,256]{1,0:T(8,128)(2,1)S(1)}, bf16[272,256]{1,0:T(8,128)(2,1)S(1)}, u32[]{:S(2)}, u32[]{:S(2)}) collective-permute-start(bf16[272,256]{1,0:T(8,128)(2,1)S(1)} %select_select_fusion.2.refs_0_), channel_id=1, source_target_pairs={{0,8},{1,9},{2,10},{3,11},{8,0},{9,1},{10,2},{11,3},{16,24},{17,25... | collective-permute-start | bytes 417800 | tf_op jit(solution)/shard_map/ppermute | solution.py:346
  26.5 38.1 %collective-permute-start.15 = (bf16[2,784,256]{2,1,0:T(8,128)(2,1)S(1)}, bf16[2,784,256]{2,1,0:T(8,128)(2,1)S(1)}, u32[]{:S(2)}, u32[]{:S(2)}) collective-permute-start(bf16[2,784,256]{2,1,0:T(8,128)(2,1)S(1)} %pad_maximum_fusion.rest_4_), channel_id=1, source_target_pairs={{2,3},{6,7},{10,11},{15,14},{18,19},{22,23},{26,27},{31,30}} | collective-permute-start | bytes 2408456 | tf_op jit(solution)/shard_map/ppermute | solution.py:346
  27.9 2.4 %collective-permute-start.12 = (bf16[2,784,256]{2,1,0:T(8,128)(2,1)S(1)}, bf16[2,784,256]{2,1,0:T(8,128)(2,1)S(1)}, u32[]{:S(2)}, u32[]{:S(2)}) collective-permute-start(bf16[2,784,256]{2,1,0:T(8,128)(2,1)S(1)} %pad_maximum_fusion.rest_4_), channel_id=1, source_target_pairs={{0,24},{16,8},{5,29},{21,13},{10,18},{26,2},{15,23},{31,7}} | collective-permute-start | bytes 2408456 | tf_op jit(solution)/shard_map/ppermute | solution.py:346
  28.6 1.7 %collective-permute-start.11 = (bf16[2,784,256]{2,1,0:T(8,128)(2,1)S(1)}, bf16[2,784,256]{2,1,0:T(8,128)(2,1)S(1)}, u32[]{:S(2)}, u32[]{:S(2)}) collective-permute-start(bf16[2,784,256]{2,1,0:T(8,128)(2,1)S(1)} %pad_maximum_fusion.rest_4_), channel_id=1, source_target_pairs={{0,16},{16,0},{5,21},{21,5},{10,26},{26,10},{15,31},{31,15}} | collective-permute-start | bytes 2408456 | tf_op jit(solution)/shard_map/ppermute | solution.py:346
  29.3 1.0 %collective-permute-start.10 = (bf16[2,784,256]{2,1,0:T(8,128)(2,1)S(1)}, bf16[2,784,256]{2,1,0:T(8,128)(2,1)S(1)}, u32[]{:S(2)}, u32[]{:S(2)}) collective-permute-start(bf16[2,784,256]{2,1,0:T(8,128)(2,1)S(1)} %pad_maximum_fusion.rest_4_), channel_id=1, source_target_pairs={{0,8},{16,24},{5,13},{21,29},{10,2},{26,18},{15,7},{31,23}} | collective-permute-start | bytes 2408456 | tf_op jit(solution)/shard_map/ppermute | solution.py:346
  30.3 34.3 %copy-start = (f32[3,6]{1,0:T(4,128)S(1)}, f32[3,6]{1,0:T(4,128)}, u32[]{:S(2)}) copy-start(f32[3,6]{1,0:T(4,128)} %scales.3) | copy-start | bytes 220
  30.6 34.1 %collective-permute-start.14 = (bf16[2,784,256]{2,1,0:T(8,128)(2,1)S(1)}, bf16[2,784,256]{2,1,0:T(8,128)(2,1)S(1)}, u32[]{:S(2)}, u32[]{:S(2)}) collective-permute-start(bf16[2,784,256]{2,1,0:T(8,128)(2,1)S(1)} %get-tuple-element.27.rest_1_), channel_id=1, source_target_pairs={{0,4},{2,6},{5,1},{7,3},{8,12},{10,14},{13,9},{15,11},{16,20},{18,... | collective-permute-start | bytes 2408456 | tf_op jit(solution)/shard_map/ppermute | solution.py:346
  31.9 32.8 %collective-permute-start.13 = (bf16[2,784,256]{2,1,0:T(8,128)(2,1)S(1)}, bf16[2,784,256]{2,1,0:T(8,128)(2,1)S(1)}, u32[]{:S(2)}, u32[]{:S(2)}) collective-permute-start(bf16[2,784,256]{2,1,0:T(8,128)(2,1)S(1)} %get-tuple-element.28.rest_0_), channel_id=1, source_target_pairs={{0,4},{2,6},{5,1},{7,3},{8,12},{10,14},{13,9},{15,11},{16,20},{18,... | collective-permute-start | bytes 2408456 | tf_op jit(solution)/shard_map/ppermute | solution.py:346
  33.2 31.5 %collective-permute-start.9 = (bf16[16,128,128]{2,1,0:T(8,128)(2,1)S(1)}, bf16[16,128,128]{2,1,0:T(8,128)(2,1)S(1)}, u32[]{:S(2)}, u32[]{:S(2)}) collective-permute-start(bf16[16,128,128]{2,1,0:T(8,128)(2,1)S(1)} %factor_pivots.1.factors), channel_id=1, source_target_pairs={{0,4},{1,5},{2,6},{3,7},{8,12},{9,13},{10,14},{11,15},{16,20},{17,... | collective-permute-start | bytes 1572872 | tf_op jit(solution)/shard_map/ppermute | solution.py:346
